TPU v7x, 256 devices: a whole 4x4x8 slice. The times are simulated.
256 devices in a mesh: head: 8 (over y, core), seq: 32 (over z, x).
Axes of the slice: x: 4, y: 4, z: 8, core: 2. Of those that a mesh axis runs over, the one named last changes fastest.
Arguments:
- queries: bfloat16 [32768, 2048], P('seq', 'head'), may hold values from -4 to 4
- keys: bfloat16 [32768, 2048], P('seq', 'head'), may hold values from -4 to 4
- values: bfloat16 [32768, 4096], P('seq', 'head'), may hold values from -6 to 6
- input_gate: float32 [32768, 8], P('seq', 'head'), may hold values from -4 to 4
- forget_gate: float32 [32768, 8], P('seq', 'head')
- out_weight: bfloat16 [4096, 4096], P('head', 'seq'), may hold values from -0.09375 to 0.09375
Outputs:
- mixed: bfloat16 [32768, 4096], P('seq', 'head')
All inputs are finite; a program needn't handle non-finite values.
Results may differ from a plain program's by a relative error of at most 0.019.
Values may be sent and summed in bfloat16 or wider, within the bound.
A program may use at most 128 MiB of HBM per device.

v0:
```python
import jax
import jax.numpy as jnp
from jax import lax
from jax.sharding import PartitionSpec as P

WINDOW = 1024


PRECISE = lax.Precision.HIGHEST
VERY_NEGATIVE = -1e30


def from_behind(block, axis, distance):
    devices = range(lax.axis_size(axis))
    route = [(i - distance, i) for i in devices if i - distance in devices]
    return lax.ppermute(block, axis, route)


def entering(part, axis, combine, identity):
    place = lax.axis_index(axis)
    gathered = jax.tree.map(lambda a: lax.all_gather(a, axis), part)
    state = jax.tree.map(lambda a, e: jnp.zeros_like(a) + jnp.asarray(e, a.dtype), part, identity)

    def one(hop, state):
        return combine(
            state, jax.tree.map(lambda a: lax.dynamic_index_in_dim(a, hop, 0, False), gathered)
        )

    return lax.fori_loop(0, place, one, state)


def memory_block(query_rows, key_rows, value_rows, gate_keys, cum_query, cum_key, carry_state):
    mem_c, mem_n, mem_m = carry_state
    key_scale = query_rows.shape[-1] ** (-0.5)
    scores = jnp.dot(query_rows, key_rows.T, preferred_element_type=jnp.float32) * key_scale
    query_index = jnp.arange(query_rows.shape[0], dtype=jnp.int32)
    key_index = jnp.arange(key_rows.shape[0], dtype=jnp.int32)
    causal = key_index[None, :] <= query_index[:, None]
    log_decay = jnp.where(
        causal, cum_query[:, None] - cum_key[None, :] + gate_keys[None, :], VERY_NEGATIVE
    )
    carry_log = cum_query + mem_m
    mem_max = jnp.maximum(jnp.max(log_decay, axis=1), carry_log)
    decays = jnp.where(causal, jnp.exp(log_decay - mem_max[:, None]), 0.0)
    weighted = decays * scores
    carry_scale = jnp.exp(carry_log - mem_max)
    query_full = query_rows.astype(jnp.float32) * key_scale
    numerator = jnp.dot(
        weighted.astype(jnp.bfloat16), value_rows, preferred_element_type=jnp.float32
    )
    numerator = numerator + carry_scale[:, None] * jnp.dot(query_full, mem_c, precision=PRECISE)
    denominator = jnp.sum(weighted, axis=1) + carry_scale * jnp.dot(
        query_full, mem_n, precision=PRECISE
    )
    return (numerator, denominator, mem_max)


def window_block(query_rows, key_window, value_window, query_pos, key_pos, mem_max):
    key_scale = query_rows.shape[-1] ** (-0.5)
    scores = jnp.dot(query_rows, key_window.T, preferred_element_type=jnp.float32) * key_scale
    visible = (
        (key_pos[None, :] <= query_pos[:, None])
        & (key_pos[None, :] > query_pos[:, None] - WINDOW)
        & (key_pos[None, :] >= 0)
    )
    top_score = jnp.max(jnp.where(visible, scores, VERY_NEGATIVE), axis=1)
    joint_max = jnp.maximum(top_score, mem_max)
    weights = jnp.where(visible, jnp.exp(scores - joint_max[:, None]), 0.0)
    numerator = jnp.dot(
        weights.astype(jnp.bfloat16), value_window, preferred_element_type=jnp.float32
    )
    return (numerator, jnp.sum(weights, axis=1), joint_max)


def joint_output(window, memory):
    win_num, win_den, joint_max = window
    mem_num, mem_den, mem_max = memory
    lifted = jnp.exp(mem_max - joint_max)
    bottom = win_den + lifted * jnp.maximum(jnp.abs(mem_den), 1.0)
    return ((win_num + lifted[:, None] * mem_num) / bottom[:, None]).astype(jnp.bfloat16)


def span_summary(key_rows, value_rows, gate_keys, cum_key):
    total_decay = cum_key[-1]
    log_weight = total_decay - cum_key + gate_keys
    new_max = jnp.max(log_weight)
    scaled_keys = key_rows.astype(jnp.float32) * jnp.exp(log_weight - new_max)[:, None]
    mem_c = jnp.dot(scaled_keys.T, value_rows.astype(jnp.float32), precision=PRECISE)
    return (mem_c, jnp.sum(scaled_keys, axis=0), new_max, total_decay)


def merge_states(older, newer):
    lifted = newer[3] + older[2]
    new_max = jnp.maximum(lifted, newer[2])
    old_weight = jnp.exp(lifted - new_max)
    new_weight = jnp.exp(newer[2] - new_max)
    mem_c = old_weight[..., None, None] * older[0] + new_weight[..., None, None] * newer[0]
    mem_n = old_weight[..., None] * older[1] + new_weight[..., None] * newer[1]
    return (mem_c, mem_n, new_max, older[3] + newer[3])


def split_heads(matrix, head_count):
    return matrix.reshape(matrix.shape[0], head_count, matrix.shape[1] // head_count).transpose(
        1, 0, 2
    )


def local(queries, keys, values, input_gate, forget_gate, out_weight):
    row_count = queries.shape[0]
    local_heads = input_gate.shape[1]
    tail_pair = (keys, values)
    pieces = [from_behind((tail_pair[0], tail_pair[1]), "seq", 1)]
    ext_keys = jnp.concatenate([entry[0] for entry in pieces[::-1]] + [keys], axis=0)
    ext_values = jnp.concatenate([entry[1] for entry in pieces[::-1]] + [values], axis=0)
    query_heads = split_heads(queries, local_heads)
    key_heads = split_heads(keys, local_heads)
    value_heads = split_heads(values, local_heads)
    ext_key_heads = split_heads(ext_keys, local_heads)
    ext_value_heads = split_heads(ext_values, local_heads)
    gate_heads = input_gate.T
    cum_heads = jnp.cumsum(jax.nn.log_sigmoid(forget_gate.T), axis=1)
    summaries = jax.vmap(span_summary)(key_heads, value_heads, gate_heads, cum_heads)
    identity = (
        jnp.zeros_like(summaries[0]),
        jnp.zeros_like(summaries[1]),
        jnp.full_like(summaries[2], VERY_NEGATIVE),
        jnp.zeros_like(summaries[3]),
    )
    carried = entering(summaries, "seq", merge_states, identity)
    base_pos = lax.axis_index("seq") * row_count
    block_rows = min(row_count, 512)

    def head_output(
        query_all, key_all, value_all, key_ext, value_ext, gate_keys, cum_gate, mem_c, mem_n, mem_m
    ):
        results = []
        state = (mem_c, mem_n, mem_m, jnp.zeros_like(mem_m))
        for block_index in range(row_count // block_rows):
            first_row = block_index * block_rows
            last_row = first_row + block_rows
            query_rows = query_all[first_row:last_row]
            key_rows = key_all[first_row:last_row]
            value_rows = value_all[first_row:last_row]
            gate_rows = gate_keys[first_row:last_row]
            local_cum = cum_gate[first_row:last_row]
            if first_row > 0:
                local_cum = local_cum - cum_gate[first_row - 1]
            memory = memory_block(
                query_rows, key_rows, value_rows, gate_rows, local_cum, local_cum, state[:3]
            )
            key_window = key_ext[first_row : last_row + WINDOW]
            value_window = value_ext[first_row : last_row + WINDOW]
            query_pos = base_pos + first_row + jnp.arange(block_rows, dtype=jnp.int32)
            key_pos = (
                base_pos + first_row - WINDOW + jnp.arange(WINDOW + block_rows, dtype=jnp.int32)
            )
            window = window_block(
                query_rows, key_window, value_window, query_pos, key_pos, memory[2]
            )
            results.append(joint_output(window, memory))
            if last_row < row_count:
                state = merge_states(
                    state, span_summary(key_rows, value_rows, gate_rows, local_cum)
                )
        return jnp.concatenate(results, axis=0)

    hidden_heads = jax.vmap(head_output)(
        query_heads,
        key_heads,
        value_heads,
        ext_key_heads,
        ext_value_heads,
        gate_heads,
        cum_heads,
        carried[0],
        carried[1],
        carried[2],
    )
    hidden = hidden_heads.transpose(1, 0, 2).reshape(row_count, local_heads * hidden_heads.shape[2])
    partial_terms = jnp.dot(
        hidden,
        lax.all_gather(out_weight, "seq", axis=1, tiled=True),
        preferred_element_type=jnp.float32,
    )
    mixed = lax.psum_scatter(
        partial_terms.astype(jnp.bfloat16), "head", scatter_dimension=1, tiled=True
    )
    return mixed


def solution(mesh):
    placed = (
        P("seq", "head"),
        P("seq", "head"),
        P("seq", "head"),
        P("seq", "head"),
        P("seq", "head"),
        P("head", "seq"),
    )
    return jax.shard_map(
        local, mesh=mesh, in_specs=placed, out_specs=P("seq", "head"), check_vma=False
    )
```

profile of v0, /device:TPU:1, one launch (start us, length us, event | category | flops | bytes accessed | tf_op | source)
XLA Modules:
  0.0 400.4 jit_solution(119145561673392502)
XLA Ops:
  6.5 0.8 neg.43
  8.1 0.7 fusion.103
  8.7 1.9 add_reduce_fusion
  10.7 2.0 fusion.89
  12.6 3.5 fusion.42
  16.3 4.0 collective-permute-start
  20.2 3.2 collective-permute-start.1
  23.6 0.7 slice.80
  24.2 1.2 dynamic-slice
  25.5 1.2 bitcast_dynamic-update-slice_fusion
  26.7 1.3 dynamic-update-slice.1
  28.0 97.5 %all-reduce.2 = (f32[32]{0:T(128)S(1)}, f32[32]{0:T(128)S(1)}) all-reduce(f32[32]{0:T(128)S(1)} %bitcast_dynamic-update-slice_fusion, f32[32]{0:T(128)S(1)} %dynamic-update-slice.1), channel_id=1, replica_groups=mesh['head'=8,'seq'=32] {'seq'}, use_global_device_ids=true, to_apply=%add | all-reduce | flops 64 | bytes 512
  126.0 41.6 %all-gather.2 = f32[32,1,256]{2,1,0:T(1,128)S(1)} all-gather(f32[1,1,256]{2,1,0:T(1,128)S(1)} %bitcast.249), channel_id=3, replica_groups=mesh['head'=8,'seq'=32] {'seq'}, dimensions={0}, use_global_device_ids=true | all-gather | bytes 33792 | tf_op jit(solution)/shard_map/all_gather | solution.py:21
  167.7 3.0 select_reduce_fusion.1
  170.8 3.0 select_reduce_fusion
  173.8 1.4 maximum_bitcast_fusion
  176.4 0.8 subtract_exponential_fusion.4
  177.2 1.3 fusion.102
  179.8 0.7 subtract_exponential_fusion
  180.9 0.8 fusion.28
  182.2 1.5 fusion.2
  183.7 0.6 fusion.38
  184.7 1.5 fusion.4
  186.2 0.6 fusion.33
  186.8 0.5 fusion.62
  187.8 1.1 fusion.17
  188.9 1.1 fusion.15
  190.0 1.9 fusion.50
  191.9 1.8 fusion.45
  193.7 60.6 %all-gather.6.cloned.1.call-done = bf16[512,4096]{1,0:T(8,128)(2,1)} async-done(((bf16[512,128]{1,0:T(8,128)(2,1)}), bf16[512,4096]{1,0:T(8,128)(2,1)}) %all-gather.6.cloned.1.call-update) | async-done | bytes 4194320 | tf_op jit(solution)/shard_map/all_gather | solution.py:182
  254.3 9.6 %convolution_convert_fusion = bf16[1024,4096]{1,0:T(8,128)(2,1)} fusion(bf16[512,4096]{1,0:T(8,128)(2,1)} %all-gather.6.cloned.1.call-done, bf16[1,512,512]{2,1,0:T(8,128)(2,1)S(1)} %fusion.45, bf16[1,512,512]{2,1,0:T(8,128)(2,1)S(1)} %fusion.50), kind=kOutput, calls=%fused_computation.4 | convolution fusion | flops 4301258752 | bytes 13631488 | tf_op jit(solution)/shard_map/dot_general | solution.py:180
  263.9 129.9 %reduce-scatter.2.cloned.1.call-done = bf16[1024,512]{1,0:T(8,128)(2,1)} async-done(((bf16[1024,4096]{1,0:T(8,128)(2,1)}), bf16[1024,512]{1,0:T(8,128)(2,1)}) %reduce-scatter.2.cloned.1.call-update) | async-done | bytes 1048592 | tf_op jit(solution)/shard_map/reduce_scatter | solution.py:185
  (57 shorter events, 3.5 us)
Async XLA Ops:
  6.5 119.0 %copy-start.1 = (bf16[1024,256]{1,0:T(8,128)(2,1)S(1)}, bf16[1024,256]{1,0:T(8,128)(2,1)}, u32[]{:S(2)}) copy-start(bf16[1024,256]{1,0:T(8,128)(2,1)} %param.9) | copy-start | bytes 1572868
  6.5 161.2 %copy-start.5 = (bf16[1024,256]{1,0:T(8,128)(2,1)S(1)}, bf16[1024,256]{1,0:T(8,128)(2,1)}, u32[]{:S(2)}) copy-start(bf16[1024,256]{1,0:T(8,128)(2,1)} %param.8) | copy-start | bytes 1572868
  6.5 168.7 %all-gather.8.cloned.1.call-start = ((), (), s32[]{:S(2)}) async-start(), calls=%async_computation.3 | async-start | bytes 17301504 | tf_op jit(solution)/shard_map/all_gather | solution.py:21
  16.2 238.1 %all-gather.6.cloned.1.call-start = ((), (), s32[]{:S(2)}) async-start(), calls=%async_computation.1 | async-start | bytes 4325376 | tf_op jit(solution)/shard_map/all_gather | solution.py:182
  16.3 151.4 %collective-permute-start = (bf16[1024,256]{1,0:T(8,128)(2,1)}, bf16[1024,256]{1,0:T(8,128)(2,1)S(1)}, u32[]{:S(2)}, u32[]{:S(2)}) collective-permute-start(bf16[1024,256]{1,0:T(8,128)(2,1)} %param.9), channel_id=1, source_target_pairs={{0,1},{1,2},{2,3},{3,4},{4,5},{5,6},{6,7},{7,8},{8,9},{9,10},{10,1... | collective-permute-start | bytes 1572872 | tf_op jit(solution)/shard_map/ppermute | solution.py:16
  20.2 153.6 %collective-permute-start.1 = (bf16[1024,512]{1,0:T(8,128)(2,1)}, bf16[1024,512]{1,0:T(8,128)(2,1)S(1)}, u32[]{:S(2)}, u32[]{:S(2)}) collective-permute-start(bf16[1024,512]{1,0:T(8,128)(2,1)} %param.10), channel_id=1, source_target_pairs={{0,1},{1,2},{2,3},{3,4},{4,5},{5,6},{6,7},{7,8},{8,9},{9,10},{10,1... | collective-permute-start | bytes 3145736 | tf_op jit(solution)/shard_map/ppermute | solution.py:16
  23.4 370.4 %reduce-scatter.2.cloned.1.call-start = ((), (), s32[]{:S(2)}) async-start(), calls=%async_computation.2 | async-start | bytes 9437184 | tf_op jit(solution)/shard_map/reduce_scatter | solution.py:185
  167.7 3.0 copy-start.6
  170.8 3.0 copy-start
  175.3 1.9 copy-start.8
  175.3 6.4 %copy-start.7 = (bf16[1024,256]{1,0:T(8,128)(2,1)S(1)}, bf16[1024,256]{1,0:T(8,128)(2,1)}, u32[]{:S(2)}) copy-start(bf16[1024,256]{1,0:T(8,128)(2,1)} %param.8) | copy-start | bytes 1572868
  175.5 6.6 %copy-start.3 = (f32[512,1536]{0,1:T(8,128)S(1)}, f32[512,1536]{0,1:T(8,128)}, u32[]{:S(2)}) copy-start(f32[512,1536]{0,1:T(8,128)} %get-tuple-element.156) | copy-start | bytes 9437188
  182.2 2.5 copy-start.2
  187.8 2.3 copy-start.4
Sparse Core Ops, SparseCore 0:
  16.3 158.3 all-gather.7
  177.2 77.0 all-gather.5
  264.0 129.7 reduce-scatter.1
where the time goes:
time: 403 us; the launch traced here: 400 us
  waiting for transfers between devices  191 us (47%)
  blocking collectives  139 us (34%)
  matrix products  28.8 us (7%)
  between operations  15.6 us (4%)
  other arithmetic  13.3 us (3%)
  starting transfers between devices  7.22 us (2%)
  local copies, waits for them, and re-layouts  5.45 us (1%)
    reduce_scatter x1, waiting for transfers between devices, local(): lax.psum_scatter(partial_terms.astype(jnp.bfloat16), 'head', scatter_dime...  130 us
    unnamed x1, blocking collectives  97.5 us
    all_gather x1, waiting for transfers between devices, local(): lax.all_gather(out_weight, 'seq', axis=1, tiled=True)  60.6 us
    all_gather x1, blocking collectives, entering(): gathered = jax.tree.map(lambda a: lax.all_gather(a, axis), part)  41.6 us
    dot_general x1, matrix products, local(): jnp.dot(hidden, lax.all_gather(out_weight, 'seq', axis=1, tiled=True), pr...  9.6 us
  transfers between devices with their start and end apart: 5, of which 2 were waited for; matrix products, arithmetic and copies ran while one was open for 7% of the time, Pallas kernels for 0%

commit v1 on v0

v1 whole, which is shorter than its diff:
```python
import functools

import jax
import jax.numpy as jnp
from jax import lax
from jax.experimental import pallas as pl
from jax.experimental.pallas import tpu as pltpu
from jax.sharding import PartitionSpec as P

MESH = pl.DeviceIdType.MESH
NEG = -1e30
F32 = jnp.float32
BF16 = jnp.bfloat16

ROWS = 1024
DK = 256
DV = 512
CH = 256
NCH = ROWS // CH
HEADS = 8
SEQ = 32
NZ = 8
NX = 4
SL = 16


def nt(a, b):
    return lax.dot_general(a, b, (((1,), (1,)), ((), ())), preferred_element_type=F32)


def nn(a, b):
    return jnp.dot(a, b, preferred_element_type=F32)


def kernel(
    q_ref, k_ref, v_ref, ig_ref, fg_ref, w_ref, out_ref,
    kp, vp, wbuf, hid, num, cflat, crecv, csend, cpre, meta,
    cumc, mml, xs, aw, bw, carried,
    kv_s, kv_r, w0_s, w0_r, wx_s, wx_r, wz_s, wz_r, sc_s, sc_r, h_s, h_r,
):
    h = lax.axis_index("head")
    s = lax.axis_index("seq")
    z, x = s // NX, s % NX
    y, core = h // 2, h % 2
    mate = y * 2 + (1 - core)
    up = ((y + 1) % 4) * 2 + core
    down = ((y + 3) % 4) * 2 + core
    across = ((y + 2) % 4) * 2 + core
    z_up = ((z + 1) % NZ) * NX + x
    z_down = ((z + NZ - 1) % NZ) * NX + x

    def remote(src, dst, ss, rs, dev):
        return pltpu.make_async_remote_copy(
            src_ref=src, dst_ref=dst, send_sem=ss, recv_sem=rs, device_id=dev, device_id_type=MESH
        )

    barrier = pltpu.get_barrier_semaphore()

    def greet(dev):
        pl.semaphore_signal(barrier, inc=1, device_id=dev, device_id_type=MESH)

    def greet_seq(k, c):
        greet((h, (s + k) % SEQ))
        return c

    lax.fori_loop(1, SEQ, greet_seq, 0)
    greet((mate, s))
    greet((up, s))
    greet((down, s))
    off_diag = z != h

    @pl.when(off_diag)
    def _():
        greet((z, h * NX + x))

    pl.semaphore_wait(barrier, SEQ - 1 + 3 + jnp.where(off_diag, 1, 0))

    def kv_copies(c):
        rows = pl.ds(c * CH, CH)
        to = (h, (s + 1) % SEQ)
        return (
            remote(k_ref.at[rows], kp.at[rows], kv_s.at[c, 0], kv_r.at[c, 0], to),
            remote(v_ref.at[rows], vp.at[rows], kv_s.at[c, 1], kv_r.at[c, 1], to),
        )

    for c in reversed(range(NCH)):
        for d in kv_copies(c):
            d.start()

    def w_block(row_block, col):
        return wbuf.at[row_block, :, pl.ds(pl.multiple_of(col * 128, 128), 128)]

    w0 = remote(w_ref, w_block(h, x), w0_s, w0_r, (z, h * NX + x))

    @pl.when(off_diag)
    def _():
        w0.start()

    @pl.when(jnp.logical_not(off_diag))
    def _():
        wbuf[z, :, pl.ds(pl.multiple_of(x * 128, 128), 128)] = w_ref[...]

    f_row = fg_ref[...]
    lf = jnp.minimum(f_row, 0.0) - jnp.log1p(jnp.exp(-jnp.abs(f_row)))
    lf8 = jnp.concatenate([lf[:, k * 128 : (k + 1) * 128] for k in range(8)], axis=0)
    tri = (
        lax.broadcasted_iota(jnp.int32, (128, 128), 0)
        <= lax.broadcasted_iota(jnp.int32, (128, 128), 1)
    ).astype(F32)
    part = jnp.dot(lf8, tri, precision=lax.Precision.HIGHEST, preferred_element_type=F32)
    pieces = []
    offset = jnp.zeros((1, 1), F32)
    for k in range(8):
        pieces.append(part[k : k + 1, :] + offset)
        offset = offset + part[k : k + 1, 127:128]
    cum_row = jnp.concatenate(pieces, axis=1)
    total = offset
    u_row = ig_ref[...] - cum_row
    u_max = jnp.max(u_row, axis=1, keepdims=True)
    w_row = jnp.exp(u_row - u_max)
    cumc[...] = jnp.transpose(jnp.broadcast_to(cum_row, (128, ROWS)))
    w_col = jnp.transpose(jnp.broadcast_to(w_row, (128, ROWS)))[:, 0:1]

    kw = k_ref[...].astype(F32) * w_col
    n_own = jnp.sum(kw, axis=0, keepdims=True)
    kw_t = jnp.transpose(kw).astype(BF16)
    cflat[0:DK, :] = nn(kw_t, v_ref[:, 0 : DV // 2]).astype(BF16)
    cflat[DK : 2 * DK, :] = nn(kw_t, v_ref[:, DV // 2 : DV]).astype(BF16)
    meta[s] = jnp.concatenate(
        [
            jnp.broadcast_to(total, (1, 128)),
            jnp.broadcast_to(total + u_max, (1, 128)),
            n_own[:, 0:128],
            n_own[:, 128:256],
            jnp.zeros((4, 128), F32),
        ],
        axis=0,
    )

    def piece(i):
        return pl.ds(pl.multiple_of(i * SL, SL), SL)

    def send_meta(k, c):
        to = (s + k) % SEQ
        remote(meta.at[s], meta.at[s], sc_s.at[0], sc_r.at[0], (h, to)).start()
        remote(cflat.at[piece(to)], crecv.at[piece(s)], sc_s.at[1], sc_r.at[1], (h, to)).start()
        return c

    lax.fori_loop(1, SEQ, send_meta, 0)
    crecv[piece(s), :] = cflat[piece(s), :]

    def chunk_own(i):
        rows = pl.ds(i * CH, CH)
        nk = (i + 1) * CH
        q = q_ref[rows] * BF16(DK**-0.5)
        sc = nt(q, k_ref[0:nk, :])
        mask = lax.broadcasted_iota(jnp.int32, (CH, nk), 1) <= (
            lax.broadcasted_iota(jnp.int32, (CH, nk), 0) + i * CH
        )
        cum = cumc[rows, 0:1]
        u = jnp.where(mask, u_row[:, 0:nk], NEG)
        ms = jnp.where(mask, sc, NEG)
        mm = cum + jnp.max(u, axis=1, keepdims=True)
        top = jnp.maximum(jnp.max(ms, axis=1, keepdims=True), mm)
        e = jnp.exp(ms - top)
        d = jnp.exp(u + (cum - top)) * sc
        mml[rows] = jnp.broadcast_to(mm, (CH, 128))
        xs[rows] = jnp.broadcast_to(top, (CH, 128))
        aw[rows] = jnp.broadcast_to(jnp.sum(e, axis=1, keepdims=True), (CH, 128))
        bw[rows] = jnp.broadcast_to(jnp.sum(d, axis=1, keepdims=True), (CH, 128))
        num[rows] = nn((e + d).astype(BF16), v_ref[0:nk, :])

    for i in reversed(range(NCH)):
        chunk_own(i)

    @pl.when(off_diag)
    def _():
        w0.wait()

    def wx_copy(k):
        return remote(
            w_block(z, x), w_block(z, x), wx_s.at[k - 1], wx_r.at[k - 1], (h, z * NX + (x + k) % NX)
        )

    for k in range(1, NX):
        wx_copy(k).start()

    def wait_recv(ref, sem):
        pltpu.make_async_copy(ref, ref, sem).wait()

    wait_recv(meta.at[0 : SEQ - 1], sc_r.at[0])
    wait_recv(crecv.at[0 : (SEQ - 1) * SL], sc_r.at[1])

    def spread(row):
        return jnp.broadcast_to(row, (8, 128))

    def quad(t):
        t = jnp.concatenate([t, t], axis=1)
        return jnp.concatenate([t, t], axis=0)

    def one(i, st):
        p, n, m = st
        csend[piece(i), :] = p.astype(BF16)

        @pl.when(i == s)
        def _():
            carried[:, 0:128] = n
            carried[:, 128:256] = m

        row = meta[i]
        f_i, m_i = spread(row[0:1, :]), spread(row[1:2, :])
        m_new = jnp.maximum(f_i + m, m_i)
        a, b = jnp.exp(f_i + m - m_new), jnp.exp(m_i - m_new)
        p = quad(a) * p + quad(b) * crecv[piece(i), :].astype(F32)
        return p, a * n + b * row, m_new

    lax.fori_loop(
        0,
        SEQ,
        one,
        (jnp.zeros((SL, DV // 2), F32), jnp.zeros((8, 128), F32), jnp.full((8, 128), NEG, F32)),
    )

    def send_prefix(k, c):
        to = (s + k) % SEQ
        remote(csend.at[piece(to)], cpre.at[piece(s)], sc_s.at[2], sc_r.at[2], (h, to)).start()
        return c

    lax.fori_loop(1, SEQ, send_prefix, 0)
    cpre[piece(s), :] = csend[piece(s), :]

    for k in range(1, NX):
        wx_copy(k).wait()

    def wz_copy(step, way):
        dev = (h, (z_up, z_down)[way])
        block = wbuf.at[(z + (NZ - step, step)[way]) % NZ]
        if step == 3:
            block = block.at[pl.ds(way * (DV // 2), DV // 2)]
        return remote(block, block, wz_s.at[way, step], wz_r.at[way, step], dev)

    wz_copy(0, 0).start()
    wz_copy(0, 1).start()

    def wz_next(step):
        for way in (0, 1):
            wz_copy(step - 1, way).wait_recv()
            if step <= 3:
                wz_copy(step, way).start()

    def h_copy(kind, c):
        half = CH // 2
        top, bottom, whole = pl.ds(c * CH, half), pl.ds(c * CH + half, half), pl.ds(c * CH, CH)
        owner, rows, to = {
            "up": (h, whole, up),
            "down": (h, whole, down),
            "mate": (h, whole, mate),
            "up2": (down, top, up),
            "down2": (up, bottom, down),
            "mate_d": (down, whole, mate),
            "mate_u": (up, whole, mate),
            "mate_t": (across, top, mate),
            "mate_b": (across, bottom, mate),
        }[kind]
        k = KINDS.index(kind)
        block = hid.at[owner, rows]
        return remote(block, block, h_s.at[k, c], h_r.at[k, c], (to, s))

    def start(c, *kinds):
        for kind in kinds:
            h_copy(kind, c).start()

    def got(c, *kinds):
        for kind in kinds:
            h_copy(kind, c).wait_recv()

    def chunk_rest(i):
        rows = pl.ds(i * CH, CH)
        nk = ROWS - i * CH
        q = q_ref[rows] * BF16(DK**-0.5)
        sc = nt(q, kp[i * CH : ROWS, :])
        mask = lax.broadcasted_iota(jnp.int32, (CH, nk), 1) > lax.broadcasted_iota(
            jnp.int32, (CH, nk), 0
        )
        mask = jnp.logical_and(mask, s > 0)
        ms = jnp.where(mask, sc, NEG)
        carry = cumc[rows, 0:1] + carried[0:1, 128:129]
        top1 = xs[rows, 0:1]
        top = jnp.maximum(jnp.maximum(top1, jnp.max(ms, axis=1, keepdims=True)), carry)
        e = jnp.exp(ms - top)
        a = jnp.exp(top1 - top)
        cs = jnp.exp(carry - top)
        n_row = jnp.concatenate([carried[2:3, 0:128], carried[3:4, 0:128]], axis=1)
        qn = jnp.sum(q.astype(F32) * n_row, axis=1, keepdims=True)
        den_w = aw[rows, 0:1] * a + jnp.sum(e, axis=1, keepdims=True)
        den_m = bw[rows, 0:1] * a + cs * qn
        floor = jnp.exp(jnp.maximum(mml[rows, 0:1], carry) - top)
        qc = jnp.concatenate([nn(q, cpre[0:DK, :]), nn(q, cpre[DK : 2 * DK, :])], axis=1)
        n = num[rows] * a + nn(e.astype(BF16), vp[i * CH : ROWS, :]) + cs * qc
        hid[h, rows] = (n / (den_w + jnp.maximum(jnp.abs(den_m), floor))).astype(BF16)

    def project(i):
        rows = pl.ds(i * CH, CH)
        acc = nn(hid[0, rows], wbuf[0])
        for b in range(1, HEADS):
            acc = acc + nn(hid[b, rows], wbuf[b])
        out_ref[rows] = acc.astype(BF16)

    def forward1(c):
        got(c, "up", "down")
        start(c, "up2", "down2", "mate_d", "mate_u")

    def forward2(c):
        got(c, "up2", "down2")
        start(c, "mate_t", "mate_b")

    wait_recv(cpre.at[0 : (SEQ - 1) * SL], sc_r.at[2])
    for c in (3, 2, 1, 0):
        for d in kv_copies(c):
            d.wait_recv()
        chunk_rest(c)
        start(c, "up", "down", "mate")
        wz_next({3: 1, 2: 2, 1: 3, 0: 4}[c])
        if c < 3:
            forward1(c + 1)
        if c < 2:
            forward2(c + 2)
    forward1(0)
    forward2(1)
    for c in (3, 2, 1):
        got(c, "mate", "mate_d", "mate_u", "mate_t", "mate_b")
        project(c)
        if c == 3:
            forward2(0)
    got(0, "mate", "mate_d", "mate_u", "mate_t", "mate_b")
    project(0)

    for c in range(NCH):
        for d in kv_copies(c):
            d.wait_send()
        for kind in KINDS:
            h_copy(kind, c).wait_send()
    for step in range(4):
        wz_copy(step, 0).wait_send()
        wz_copy(step, 1).wait_send()
    wait_recv(meta.at[0 : SEQ - 1], sc_s.at[0])
    wait_recv(crecv.at[0 : (SEQ - 1) * SL], sc_s.at[1])
    wait_recv(crecv.at[0 : (SEQ - 1) * SL], sc_s.at[2])


KINDS = ("up", "down", "mate", "up2", "down2", "mate_d", "mate_u", "mate_t", "mate_b")


def local(queries, keys, values, input_gate, forget_gate, out_weight):
    dma = pltpu.SemaphoreType.DMA
    vmem = pl.BlockSpec(memory_space=pltpu.VMEM)
    return pl.pallas_call(
        kernel,
        out_shape=jax.ShapeDtypeStruct((ROWS, DV), BF16),
        in_specs=[vmem] * 6,
        out_specs=vmem,
        scratch_shapes=[
            pltpu.VMEM((ROWS, DK), BF16),
            pltpu.VMEM((ROWS, DV), BF16),
            pltpu.VMEM((HEADS, DV, DV), BF16),
            pltpu.VMEM((HEADS, ROWS, DV), BF16),
            pltpu.VMEM((ROWS, DV), F32),
            pltpu.VMEM((2 * DK, DV // 2), BF16),
            pltpu.VMEM((2 * DK, DV // 2), BF16),
            pltpu.VMEM((2 * DK, DV // 2), BF16),
            pltpu.VMEM((2 * DK, DV // 2), BF16),
            pltpu.VMEM((SEQ, 8, 128), F32),
            pltpu.VMEM((ROWS, 128), F32),
            pltpu.VMEM((ROWS, 128), F32),
            pltpu.VMEM((ROWS, 128), F32),
            pltpu.VMEM((ROWS, 128), F32),
            pltpu.VMEM((ROWS, 128), F32),
            pltpu.VMEM((8, DK), F32),
            dma((NCH, 2)), dma((NCH, 2)),
            dma, dma,
            dma((NX - 1,)), dma((NX - 1,)),
            dma((2, 4)), dma((2, 4)),
            dma((3,)), dma((3,)),
            dma((len(KINDS), NCH)), dma((len(KINDS), NCH)),
        ],
        compiler_params=pltpu.CompilerParams(
            collective_id=0, has_side_effects=True, vmem_limit_bytes=56 << 20
        ),
        cost_estimate=pl.CostEstimate(
            flops=8 * 10**9, bytes_accessed=4 << 20, transcendentals=4 << 20
        ),
    )(queries, keys, values, input_gate.T, forget_gate.T, out_weight)


def solution(mesh):
    placed = (
        P("seq", "head"),
        P("seq", "head"),
        P("seq", "head"),
        P("seq", "head"),
        P("seq", "head"),
        P("head", "seq"),
    )
    return jax.shard_map(
        local, mesh=mesh, in_specs=placed, out_specs=P("seq", "head"), check_vma=False
    )
```

time: 403 us -> 134 us (0.33)
  waiting for transfers between devices: 191 us -> 0 us
  blocking collectives: 139 us -> 0 us
  Pallas kernels: 0 us -> 131 us
  matrix products: 28.8 us -> 0 us
  between operations: 15.6 us -> 0.01 us
  other arithmetic: 13.3 us -> 0 us
  starting transfers between devices: 7.22 us -> 0 us
    pallas_call x0 -> x1, Pallas kernels: none -> 131 us  [local(): pl.pallas_call(kernel, out_shape=jax.ShapeDtypeStruct((ROWS, DV), BF16),...]
    reduce_scatter x1 -> x0, waiting for transfers between devices: 130 us -> none  [local(): lax.psum_scatter(partial_terms.astype(jnp.bfloat16), 'head', scatter_dime...]
    unnamed x1 -> x0, blocking collectives: 97.5 us -> none
    all_gather x2 -> x0, waiting for transfers between devices: 60.6 us -> none  [the longest x1 60.6 us: local(): lax.all_gather(out_weight, 'seq', axis=1, tiled=True)]
    all_gather x1 -> x0, blocking collectives: 41.6 us -> none  [entering(): gathered = jax.tree.map(lambda a: lax.all_gather(a, axis), part)]
    dot_general x15 -> x0, matrix products: 28.8 us -> none  [the longest x1 9.6 us: local(): jnp.dot(hidden, lax.all_gather(out_weight, 'seq', axis=1, tiled=True), pr...]
    ppermute x2 -> x0, starting transfers between devices: 7.13 us -> none  [from_behind(): return lax.ppermute(block, axis, route)]
  transfers between devices with their start and end apart: 5 -> 0, of which waited for: 2 -> 0; matrix products, arithmetic and copies ran while one was open for 7% -> 0% of each run, Pallas kernels for 0% -> 0%
where the time goes in v1:
time: 134 us; the launch traced here: 133 us
  Pallas kernels  131 us (98%)
  local copies, waits for them, and re-layouts  2.26 us (2%)
    pallas_call x1, Pallas kernels, local(): pl.pallas_call(kernel, out_shape=jax.ShapeDtypeStruct((ROWS, DV), BF16),...  131 us

profile of v1, /device:TPU:1, one launch (start us, length us, event | category | flops | bytes accessed | tf_op | source)
XLA Modules:
  0.0 133.0 jit_solution(4384343645846337383)
XLA Ops:
  0.0 130.7 %shard_map.64 = bf16[1024,512]{1,0:T(8,128)(2,1)} custom-call(bf16[1024,256]{1,0:T(8,128)(2,1)} %q_ref.1, bf16[1024,256]{1,0:T(8,128)(2,1)} %k_ref.1, bf16[1024,512]{1,0:T(8,128)(2,1)} %v_ref.1, f32[1,1024]{1,0:T(1,128)} %bitcast.2, f32[1,1024]{1,0:T(1,128)} %bitcast.3, bf16[512,128]{1,0:T(8,128)(2,1)} %w_ref.1), custom_call_target="tpu_custom_call" | custom-call | flops 8000000000 | bytes 4194304 | tf_op jit(solution)/shard_map/pallas_call | solution.py:357
  130.7 2.3 %copy.8 = bf16[1024,512]{1,0:T(8,128)(2,1)} copy(bf16[1024,512]{1,0:T(8,128)(2,1)} %shard_map.64) | data formatting | bytes 2097152

commit v2 on v1

--- a/solution.py
+++ b/solution.py
@@ -21,7 +21,8 @@
 SEQ = 32
 NZ = 8
 NX = 4
-SL = 16
+QR = 2 * DK // NX
+SL = QR // NZ
 
 
 def nt(a, b):
@@ -34,9 +35,11 @@
 
 def kernel(
     q_ref, k_ref, v_ref, ig_ref, fg_ref, w_ref, out_ref,
-    kp, vp, wbuf, hid, num, cflat, crecv, csend, cpre, meta,
+    kp, vp, wbuf, hid, num, cflat, cx, ctot, cz, csend, zpre, csend2, cpre, metax, metaz,
     cumc, mml, xs, aw, bw, carried,
-    kv_s, kv_r, w0_s, w0_r, wx_s, wx_r, wz_s, wz_r, sc_s, sc_r, h_s, h_r,
+    kv_s, kv_r,  w0_s, w0_r, ax_s, ax_r, bz_s, bz_r,
+    al_s, al_r, ar_s, ar_r, bl_s, bl_r, br_s, br_r,
+    mx_s, mx_r, cx_s, cx_r, px_s, px_r, mz_s, mz_r, cz_s, cz_r, pz_s, pz_r, h_s, h_r,
 ):
     h = lax.axis_index("head")
     s = lax.axis_index("seq")
@@ -59,21 +62,29 @@
     def greet(dev):
         pl.semaphore_signal(barrier, inc=1, device_id=dev, device_id_type=MESH)
 
-    def greet_seq(k, c):
-        greet((h, (s + k) % SEQ))
-        return c
-
-    lax.fori_loop(1, SEQ, greet_seq, 0)
+    for k in range(1, NX):
+        greet((h, z * NX + (x + k) % NX))
+    for k in range(1, NZ):
+        greet((h, (z + k) % NZ * NX + x))
     greet((mate, s))
     greet((up, s))
     greet((down, s))
     off_diag = z != h
+    first, last = x == 0, x == NX - 1
 
     @pl.when(off_diag)
     def _():
         greet((z, h * NX + x))
 
-    pl.semaphore_wait(barrier, SEQ - 1 + 3 + jnp.where(off_diag, 1, 0))
+    @pl.when(last)
+    def _():
+        greet((h, (s + 1) % SEQ))
+
+    @pl.when(first)
+    def _():
+        greet((h, (s + SEQ - 1) % SEQ))
+
+    greeted = NX - 1 + NZ - 1 + 3 + jnp.where(off_diag, 1, 0) + jnp.where(first | last, 1, 0)
 
     def kv_copies(c):
         rows = pl.ds(c * CH, CH)
@@ -83,7 +94,10 @@
             remote(v_ref.at[rows], vp.at[rows], kv_s.at[c, 1], kv_r.at[c, 1], to),
         )
 
-    for c in reversed(range(NCH)):
+    def kv_first():
+        pass
+
+    def kv_start(c):
         for d in kv_copies(c):
             d.start()
 
@@ -91,10 +105,6 @@
         return wbuf.at[row_block, :, pl.ds(pl.multiple_of(col * 128, 128), 128)]
 
     w0 = remote(w_ref, w_block(h, x), w0_s, w0_r, (z, h * NX + x))
-
-    @pl.when(off_diag)
-    def _():
-        w0.start()
 
     @pl.when(jnp.logical_not(off_diag))
     def _():
@@ -126,7 +136,7 @@
     kw_t = jnp.transpose(kw).astype(BF16)
     cflat[0:DK, :] = nn(kw_t, v_ref[:, 0 : DV // 2]).astype(BF16)
     cflat[DK : 2 * DK, :] = nn(kw_t, v_ref[:, DV // 2 : DV]).astype(BF16)
-    meta[s] = jnp.concatenate(
+    metax[x] = jnp.concatenate(
         [
             jnp.broadcast_to(total, (1, 128)),
             jnp.broadcast_to(total + u_max, (1, 128)),
@@ -136,18 +146,59 @@
         ],
         axis=0,
     )
-
-    def piece(i):
-        return pl.ds(pl.multiple_of(i * SL, SL), SL)
-
-    def send_meta(k, c):
-        to = (s + k) % SEQ
-        remote(meta.at[s], meta.at[s], sc_s.at[0], sc_r.at[0], (h, to)).start()
-        remote(cflat.at[piece(to)], crecv.at[piece(s)], sc_s.at[1], sc_r.at[1], (h, to)).start()
-        return c
-
-    lax.fori_loop(1, SEQ, send_meta, 0)
-    crecv[piece(s), :] = cflat[piece(s), :]
+    pl.semaphore_wait(barrier, greeted)
+
+    def part_of(i, rows):
+        return pl.ds(pl.multiple_of(i * rows, rows), rows)
+
+    def to_x(k):
+        return (x + k) % NX
+
+    def to_z(k):
+        return (z + k) % NZ
+
+    def mx_copy(k):
+        dev = (h, z * NX + to_x(k))
+        return remote(metax.at[x], metax.at[x], mx_s.at[k - 1], mx_r.at[k - 1], dev)
+
+    def cx_copy(k):
+        dev = (h, z * NX + to_x(k))
+        return remote(
+            cflat.at[part_of(to_x(k), QR)], cx.at[part_of(x, QR)], cx_s.at[k - 1], cx_r.at[k - 1], dev
+        )
+
+    def mz_copy(k):
+        dev = (h, to_z(k) * NX + x)
+        return remote(metaz.at[z], metaz.at[z], mz_s.at[k - 1], mz_r.at[k - 1], dev)
+
+    def cz_copy(k):
+        dev = (h, to_z(k) * NX + x)
+        return remote(
+            ctot.at[part_of(to_z(k), SL)], cz.at[part_of(z, SL)], cz_s.at[k - 1], cz_r.at[k - 1], dev
+        )
+
+    def pz_copy(k):
+        dev = (h, to_z(k) * NX + x)
+        return remote(
+            csend.at[part_of(to_z(k), SL)], zpre.at[part_of(z, SL)], pz_s.at[k - 1], pz_r.at[k - 1], dev
+        )
+
+    def px_copy(k):
+        dev = (h, z * NX + to_x(k))
+        return remote(
+            csend2.at[part_of(to_x(k), QR)], cpre.at[part_of(x, QR)], px_s.at[k - 1], px_r.at[k - 1], dev
+        )
+
+    for k in range(1, NX):
+        mx_copy(k).start()
+        cx_copy(k).start()
+    kv_first()
+
+    @pl.when(off_diag)
+    def _():
+        w0.start()
+
+    cx[part_of(x, QR), :] = cflat[part_of(x, QR), :]
 
     def chunk_own(i):
         rows = pl.ds(i * CH, CH)
@@ -173,80 +224,117 @@
     for i in reversed(range(NCH)):
         chunk_own(i)
 
+    half_a, half_b = pl.ds(0, DV // 2), pl.ds(DV // 2, DV // 2)
+
+    def strip(col):
+        return pl.ds(pl.multiple_of(col * 128, 128), 128)
+
+    def ax_copy(k):
+        piece_a = wbuf.at[z, half_a, strip(x)]
+        return remote(piece_a, piece_a, ax_s.at[k - 1], ax_r.at[k - 1], (h, z * NX + (x + k) % NX))
+
+    def bz_copy(k):
+        piece_b = wbuf.at[z, half_b, strip(x)]
+        return remote(piece_b, piece_b, bz_s.at[k - 1], bz_r.at[k - 1], (h, (z + k) % NZ * NX + x))
+
+    def a_left(step):
+        block = wbuf.at[(z + step) % NZ, half_a]
+        return remote(block, block, al_s.at[step], al_r.at[step], (h, z_down))
+
+    def a_right(step):
+        block = wbuf.at[(z + NZ - step) % NZ, half_a]
+        return remote(block, block, ar_s.at[step], ar_r.at[step], (h, z_up))
+
+    def b_left(step):
+        block = wbuf.at[:, half_b, strip((x + step) % NX)]
+        return remote(block, block, bl_s.at[step], bl_r.at[step], (h, z * NX + (x + NX - 1) % NX))
+
+    def b_right(step):
+        block = wbuf.at[:, half_b, strip((x + NX - step) % NX)]
+        return remote(block, block, br_s.at[step], br_r.at[step], (h, z * NX + (x + 1) % NX))
+
+    def onward(ring, step):
+        if step:
+            ring(step - 1).wait_recv()
+        ring(step).start()
+
+    def spread(row):
+        return jnp.broadcast_to(row, (8, 128))
+
+    def wide(t):
+        return jnp.concatenate([t[0:1, :], t[0:1, :]], axis=1)
+
+    def merged(state, tile, block):
+        p, n, m = state
+        f_i, m_i = spread(tile[0:1, :]), spread(tile[1:2, :])
+        m_new = jnp.maximum(f_i + m, m_i)
+        a, b = jnp.exp(f_i + m - m_new), jnp.exp(m_i - m_new)
+        return wide(a) * p + wide(b) * block.astype(F32), a * n + b * tile, m_new
+
+    for k in range(1, NX):
+        mx_copy(k).wait_recv()
+        cx_copy(k).wait_recv()
+    empty = jnp.zeros((8, 128), F32), jnp.full((8, 128), NEG, F32)
+    state = (jnp.zeros((QR, DV // 2), F32), *empty)
+    decay = jnp.zeros((8, 128), F32)
+    for i in range(NX):
+        tile = metax[i]
+        state = merged(state, tile, cx[i * QR : (i + 1) * QR, :])
+        decay = decay + spread(tile[0:1, :])
+    ctot[...] = state[0].astype(BF16)
+    line = lax.broadcasted_iota(jnp.int32, (8, 128), 0)
+    metaz[z] = jnp.where(line == 0, decay, jnp.where(line == 1, state[2], state[1]))
+    for k in range(1, NZ):
+        mz_copy(k).start()
+        cz_copy(k).start()
+    cz[part_of(z, SL), :] = ctot[part_of(z, SL), :]
+
     @pl.when(off_diag)
     def _():
         w0.wait()
 
-    def wx_copy(k):
-        return remote(
-            w_block(z, x), w_block(z, x), wx_s.at[k - 1], wx_r.at[k - 1], (h, z * NX + (x + k) % NX)
-        )
-
-    for k in range(1, NX):
-        wx_copy(k).start()
-
-    def wait_recv(ref, sem):
-        pltpu.make_async_copy(ref, ref, sem).wait()
-
-    wait_recv(meta.at[0 : SEQ - 1], sc_r.at[0])
-    wait_recv(crecv.at[0 : (SEQ - 1) * SL], sc_r.at[1])
-
-    def spread(row):
-        return jnp.broadcast_to(row, (8, 128))
-
-    def quad(t):
-        t = jnp.concatenate([t, t], axis=1)
-        return jnp.concatenate([t, t], axis=0)
-
-    def one(i, st):
-        p, n, m = st
-        csend[piece(i), :] = p.astype(BF16)
-
-        @pl.when(i == s)
+    for k in range(1, NX):
+        ax_copy(k).start()
+
+    for k in range(1, NZ):
+        mz_copy(k).wait_recv()
+        cz_copy(k).wait_recv()
+    state = (jnp.zeros((SL, DV // 2), F32), *empty)
+    for i in range(NZ):
+        csend[i * SL : (i + 1) * SL, :] = state[0].astype(BF16)
+
+        @pl.when(z == i)
         def _():
-            carried[:, 0:128] = n
-            carried[:, 128:256] = m
-
-        row = meta[i]
-        f_i, m_i = spread(row[0:1, :]), spread(row[1:2, :])
-        m_new = jnp.maximum(f_i + m, m_i)
-        a, b = jnp.exp(f_i + m - m_new), jnp.exp(m_i - m_new)
-        p = quad(a) * p + quad(b) * crecv[piece(i), :].astype(F32)
-        return p, a * n + b * row, m_new
-
-    lax.fori_loop(
-        0,
-        SEQ,
-        one,
-        (jnp.zeros((SL, DV // 2), F32), jnp.zeros((8, 128), F32), jnp.full((8, 128), NEG, F32)),
-    )
-
-    def send_prefix(k, c):
-        to = (s + k) % SEQ
-        remote(csend.at[piece(to)], cpre.at[piece(s)], sc_s.at[2], sc_r.at[2], (h, to)).start()
-        return c
-
-    lax.fori_loop(1, SEQ, send_prefix, 0)
-    cpre[piece(s), :] = csend[piece(s), :]
-
-    for k in range(1, NX):
-        wx_copy(k).wait()
-
-    def wz_copy(step, way):
-        dev = (h, (z_up, z_down)[way])
-        block = wbuf.at[(z + (NZ - step, step)[way]) % NZ]
-        if step == 3:
-            block = block.at[pl.ds(way * (DV // 2), DV // 2)]
-        return remote(block, block, wz_s.at[way, step], wz_r.at[way, step], dev)
-
-    wz_copy(0, 0).start()
-    wz_copy(0, 1).start()
-
-    def wz_next(step):
-        for way in (0, 1):
-            wz_copy(step - 1, way).wait_recv()
-            if step <= 3:
-                wz_copy(step, way).start()
+            carried[:, 0:128] = state[1]
+            carried[:, 128:256] = state[2]
+
+        if i < NZ - 1:
+            state = merged(state, metaz[i], cz[i * SL : (i + 1) * SL, :])
+    for k in range(1, NZ):
+        pz_copy(k).start()
+    zpre[part_of(z, SL), :] = csend[part_of(z, SL), :]
+    for k in range(1, NZ):
+        bz_copy(k).start()
+    for k in range(1, NZ):
+        pz_copy(k).wait_recv()
+    state = (zpre[...].astype(F32), carried[:, 0:128], carried[:, 128:256])
+    for i in range(NX):
+        csend2[i * QR : (i + 1) * QR, :] = state[0].astype(BF16)
+
+        @pl.when(x == i)
+        def _():
+            carried[:, 0:128] = state[1]
+            carried[:, 128:256] = state[2]
+
+        if i < NX - 1:
+            state = merged(state, metax[i], cx[i * QR : (i + 1) * QR, :])
+    for k in range(1, NX):
+        px_copy(k).start()
+    kv_start(3)
+    kv_start(2)
+    kv_start(1)
+    kv_start(0)
+    cpre[part_of(x, QR), :] = csend2[part_of(x, QR), :]
 
     def h_copy(kind, c):
         half = CH // 2
@@ -314,38 +402,70 @@
         got(c, "up2", "down2")
         start(c, "mate_t", "mate_b")
 
-    wait_recv(cpre.at[0 : (SEQ - 1) * SL], sc_r.at[2])
-    for c in (3, 2, 1, 0):
+    def hidden(c):
         for d in kv_copies(c):
             d.wait_recv()
         chunk_rest(c)
         start(c, "up", "down", "mate")
-        wz_next({3: 1, 2: 2, 1: 3, 0: 4}[c])
-        if c < 3:
-            forward1(c + 1)
-        if c < 2:
-            forward2(c + 2)
+
+    for k in range(1, NX):
+        ax_copy(k).wait_recv()
+    onward(a_left, 0)
+    for k in range(1, NX):
+        px_copy(k).wait_recv()
+    hidden(3)
+    for k in range(1, NZ):
+        bz_copy(k).wait_recv()
+    onward(b_left, 0)
+    onward(a_right, 0)
+    hidden(2)
+    forward1(3)
+    onward(a_left, 1)
+    forward2(3)
+    hidden(1)
+    onward(b_right, 0)
+    forward1(2)
+    onward(b_left, 1)
+    onward(a_left, 2)
+    forward2(2)
+    hidden(0)
+    forward1(1)
+    onward(a_right, 1)
+    onward(a_left, 3)
+    forward2(1)
     forward1(0)
-    forward2(1)
-    for c in (3, 2, 1):
+    onward(a_left, 4)
+    a_right(1).wait_recv()
+    b_left(1).wait_recv()
+    b_right(0).wait_recv()
+    forward2(0)
+    a_left(4).wait_recv()
+    for c in (3, 2, 1, 0):
         got(c, "mate", "mate_d", "mate_u", "mate_t", "mate_b")
         project(c)
-        if c == 3:
-            forward2(0)
-    got(0, "mate", "mate_d", "mate_u", "mate_t", "mate_b")
-    project(0)
 
     for c in range(NCH):
         for d in kv_copies(c):
             d.wait_send()
+
+    for c in range(NCH):
         for kind in KINDS:
             h_copy(kind, c).wait_send()
-    for step in range(4):
-        wz_copy(step, 0).wait_send()
-        wz_copy(step, 1).wait_send()
-    wait_recv(meta.at[0 : SEQ - 1], sc_s.at[0])
-    wait_recv(crecv.at[0 : (SEQ - 1) * SL], sc_s.at[1])
-    wait_recv(crecv.at[0 : (SEQ - 1) * SL], sc_s.at[2])
+    for ring, steps in ((a_left, 5), (a_right, 2), (b_left, 2), (b_right, 1)):
+        for step in range(steps):
+            ring(step).wait_send()
+    for k in range(1, NX):
+        ax_copy(k).wait_send()
+    for k in range(1, NZ):
+        bz_copy(k).wait_send()
+    for k in range(1, NX):
+        mx_copy(k).wait_send()
+        cx_copy(k).wait_send()
+        px_copy(k).wait_send()
+    for k in range(1, NZ):
+        mz_copy(k).wait_send()
+        cz_copy(k).wait_send()
+        pz_copy(k).wait_send()
 
 
 KINDS = ("up", "down", "mate", "up2", "down2", "mate_d", "mate_u", "mate_t", "mate_b")
@@ -367,9 +487,14 @@
             pltpu.VMEM((ROWS, DV), F32),
             pltpu.VMEM((2 * DK, DV // 2), BF16),
             pltpu.VMEM((2 * DK, DV // 2), BF16),
+            pltpu.VMEM((QR, DV // 2), BF16),
+            pltpu.VMEM((QR, DV // 2), BF16),
+            pltpu.VMEM((QR, DV // 2), BF16),
+            pltpu.VMEM((QR, DV // 2), BF16),
             pltpu.VMEM((2 * DK, DV // 2), BF16),
             pltpu.VMEM((2 * DK, DV // 2), BF16),
-            pltpu.VMEM((SEQ, 8, 128), F32),
+            pltpu.VMEM((NX, 8, 128), F32),
+            pltpu.VMEM((NZ, 8, 128), F32),
             pltpu.VMEM((ROWS, 128), F32),
             pltpu.VMEM((ROWS, 128), F32),
             pltpu.VMEM((ROWS, 128), F32),
@@ -379,8 +504,13 @@
             dma((NCH, 2)), dma((NCH, 2)),
             dma, dma,
             dma((NX - 1,)), dma((NX - 1,)),
-            dma((2, 4)), dma((2, 4)),
-            dma((3,)), dma((3,)),
+            dma((NZ - 1,)), dma((NZ - 1,)),
+            dma((5,)), dma((5,)),
+            dma((2,)), dma((2,)),
+            dma((2,)), dma((2,)),
+            dma((1,)), dma((1,)),
+            *[dma((NX - 1,))] * 6,
+            *[dma((NZ - 1,))] * 6,
             dma((len(KINDS), NCH)), dma((len(KINDS), NCH)),
         ],
         compiler_params=pltpu.CompilerParams(

time: 134 us -> 101 us (0.75)
  Pallas kernels: 131 us -> 97.2 us
    pallas_call x1, Pallas kernels: 131 us -> 97.2 us  [local(): pl.pallas_call(kernel, out_shape=jax.ShapeDtypeStruct((ROWS, DV), BF16),...]
where the time goes in v2:
time: 101 us; the launch traced here: 99.5 us
  Pallas kernels  97.2 us (96%)
  local copies, waits for them, and re-layouts  2.26 us (2%)
    pallas_call x1, Pallas kernels, local(): pl.pallas_call(kernel, out_shape=jax.ShapeDtypeStruct((ROWS, DV), BF16),...  97.2 us
    unnamed x1, local copies, waits for them, and re-layouts  2.26 us

profile of v2, /device:TPU:1, one launch (start us, length us, event | category | flops | bytes accessed | tf_op | source)
XLA Modules:
  0.0 99.5 jit_solution(3970170271067559420)
XLA Ops:
  0.0 97.2 %shard_map.64 = bf16[1024,512]{1,0:T(8,128)(2,1)} custom-call(bf16[1024,256]{1,0:T(8,128)(2,1)} %q_ref.1, bf16[1024,256]{1,0:T(8,128)(2,1)} %k_ref.1, bf16[1024,512]{1,0:T(8,128)(2,1)} %v_ref.1, f32[1,1024]{1,0:T(1,128)} %bitcast.2, f32[1,1024]{1,0:T(1,128)} %bitcast.3, bf16[512,128]{1,0:T(8,128)(2,1)} %w_ref.1), custom_call_target="tpu_custom_call" | custom-call | flops 8000000000 | bytes 4194304 | tf_op jit(solution)/shard_map/pallas_call | solution.py:477
  97.3 2.3 %copy.8 = bf16[1024,512]{1,0:T(8,128)(2,1)} copy(bf16[1024,512]{1,0:T(8,128)(2,1)} %shard_map.64) | data formatting | bytes 2097152

commit v3 on v2

--- a/solution.py
+++ b/solution.py
@@ -387,12 +387,21 @@
         n = num[rows] * a + nn(e.astype(BF16), vp[i * CH : ROWS, :]) + cs * qc
         hid[h, rows] = (n / (den_w + jnp.maximum(jnp.abs(den_m), floor))).astype(BF16)
 
+    late = (z + 5) % NZ
+
     def project(i):
         rows = pl.ds(i * CH, CH)
-        acc = nn(hid[0, rows], wbuf[0])
-        for b in range(1, HEADS):
+        acc = nn(hid[late, rows, DV // 2 : DV], wbuf[late, DV // 2 : DV, :])
+        for k in (0, 1, 2, 3, 4, 6, 7):
+            b = (z + k) % NZ
             acc = acc + nn(hid[b, rows], wbuf[b])
-        out_ref[rows] = acc.astype(BF16)
+        num[rows] = acc
+
+    def finish(i):
+        rows = pl.ds(i * CH, CH)
+        out_ref[rows] = (
+            num[rows] + nn(hid[late, rows, 0 : DV // 2], wbuf[late, 0 : DV // 2, :])
+        ).astype(BF16)
 
     def forward1(c):
         got(c, "up", "down")
@@ -439,10 +448,12 @@
     b_left(1).wait_recv()
     b_right(0).wait_recv()
     forward2(0)
-    a_left(4).wait_recv()
     for c in (3, 2, 1, 0):
         got(c, "mate", "mate_d", "mate_u", "mate_t", "mate_b")
         project(c)
+    a_left(4).wait_recv()
+    for c in (3, 2, 1, 0):
+        finish(c)
 
     for c in range(NCH):
         for d in kv_copies(c):

time: 101 us -> 100 us (0.990); the launches traced: 99.5 us -> 99.8 us
  no operation moved by 1% of the time
where the time goes in v3:
time: 100 us; the launch traced here: 99.8 us
  Pallas kernels  97.6 us (98%)
  local copies, waits for them, and re-layouts  2.26 us (2%)
    pallas_call x1, Pallas kernels, local(): pl.pallas_call(kernel, out_shape=jax.ShapeDtypeStruct((ROWS, DV), BF16),...  97.6 us
    unnamed x1, local copies, waits for them, and re-layouts  2.26 us

profile of v3, /device:TPU:1, one launch (start us, length us, event | category | flops | bytes accessed | tf_op | source)
XLA Modules:
  0.0 99.8 jit_solution(14161895658449086550)
XLA Ops:
  0.0 97.6 %shard_map.64 = bf16[1024,512]{1,0:T(8,128)(2,1)} custom-call(bf16[1024,256]{1,0:T(8,128)(2,1)} %q_ref.1, bf16[1024,256]{1,0:T(8,128)(2,1)} %k_ref.1, bf16[1024,512]{1,0:T(8,128)(2,1)} %v_ref.1, f32[1,1024]{1,0:T(1,128)} %bitcast.2, f32[1,1024]{1,0:T(1,128)} %bitcast.3, bf16[512,128]{1,0:T(8,128)(2,1)} %w_ref.1), custom_call_target="tpu_custom_call" | custom-call | flops 8000000000 | bytes 4194304 | tf_op jit(solution)/shard_map/pallas_call | solution.py:488
  97.6 2.3 %copy.8 = bf16[1024,512]{1,0:T(8,128)(2,1)} copy(bf16[1024,512]{1,0:T(8,128)(2,1)} %shard_map.64) | data formatting | bytes 2097152
